TPU v7x, 32 devices: a whole 2x2x4 slice. The times are simulated.
32 devices in a mesh: passage: 8 (over z, y), span: 4 (over x, core).
Axes of the slice: x: 2, y: 2, z: 4, core: 2. Of those that a mesh axis runs over, the one named last changes fastest.
Arguments:
- grad_rows: float32 [16384, 3, 128], P(('passage', 'span')), may hold values from -6 to 6
- dest_rank: int32 [16384, 1], P(('passage', 'span')), may hold values from 0 to 3; in each aligned block of 512 rows (0 to 511, 512 to 1023, ...) at most 256 rows name the same one
- dest_block: int32 [16384], P(('passage', 'span')), may hold values from 0 to 255
- cell_class: int32 [64, 64, 256], P('passage', 'span'), may hold values from 0 to 15
- class_stiffness: float32 [16], replicated, may hold values from 0.05 to 1
Outputs:
- update: float32 [3, 64, 64, 256], P(None, 'passage', 'span')
Inputs may be any that keep to these rules, and one draw needn't show every extreme that they name: `dest_rank`: the rows of one device name each radial index at most 256 times, and exactly 256 times for some index of some devices.
All inputs are finite; a program needn't handle non-finite values.
Results may differ from a plain program's by a relative error of at most 0.00007.
Values sent between devices are 32-bit elements; how exact they have to be, the bound alone decides.
A program may use at most 64 MiB of HBM per device.

v0:
```python
import jax
import jax.numpy as jnp
from jax import lax
from jax.sharding import PartitionSpec as P

NPOST = 2
NCOARSE = 4


damping = 0.8
mass_share = 0.02


def extended(block, sides, width):
    for axis, dim in sides:
        count = lax.axis_size(axis)
        forward = [(i, i + 1) for i in range(count - 1)]
        forward.append((count - 1, 0))
        backward = [(target, source) for source, target in forward]
        low = lax.ppermute(
            lax.slice_in_dim(block, block.shape[dim] - width, None, axis=dim), axis, forward
        )
        high = lax.ppermute(lax.slice_in_dim(block, 0, width, axis=dim), axis, backward)
        block = jnp.concatenate([low, block, high], axis=dim)
    return block


def pair_sums(values, along):
    new_shape = list(values.shape)
    new_shape[along : along + 1] = [new_shape[along] // 2, 2]
    return values.reshape(new_shape).sum(along + 1)


def every_other(values, along, offset):
    return lax.slice_in_dim(values, offset, values.shape[along], 2, along)


def face_weights(padded):
    stiffness = padded[1:-1, 1:-1]
    along_z = jnp.pad(stiffness, ((0, 0), (0, 0), (1, 1)), mode="edge")
    return (
        stiffness + padded[:-2, 1:-1],
        stiffness + padded[2:, 1:-1],
        stiffness + padded[1:-1, :-2],
        stiffness + padded[1:-1, 2:],
        stiffness + along_z[..., :-2],
        stiffness + along_z[..., 2:],
        mass_share * stiffness,
    )


def coarsen(weights):
    lower_x, upper_x, lower_y, upper_y, lower_z, upper_z, masses = weights
    return (
        pair_sums(pair_sums(every_other(lower_x, 0, 0), 1), 2),
        pair_sums(pair_sums(every_other(upper_x, 0, 1), 1), 2),
        pair_sums(pair_sums(every_other(lower_y, 1, 0), 0), 2),
        pair_sums(pair_sums(every_other(upper_y, 1, 1), 0), 2),
        pair_sums(pair_sums(every_other(lower_z, 2, 0), 0), 1),
        pair_sums(pair_sums(every_other(upper_z, 2, 1), 0), 1),
        pair_sums(pair_sums(pair_sums(masses, 0), 1), 2),
    )


def diagonal_of(weights):
    running = weights[0]
    for member in weights[1:]:
        running = running + member
    return running


def neighbours(field, padded, weights):
    lower_x, upper_x, lower_y, upper_y, lower_z, upper_z, masses = weights
    shifted = jnp.pad(field, ((0, 0), (0, 0), (0, 0), (1, 1)))
    return (
        lower_x * padded[:, :-2, 1:-1]
        + upper_x * padded[:, 2:, 1:-1]
        + lower_y * padded[:, 1:-1, :-2]
        + upper_y * padded[:, 1:-1, 2:]
        + lower_z * shifted[..., :-2]
        + upper_z * shifted[..., 2:]
    )


def relax_once(field, source, padded, weights, diagonal):
    residue = source - (diagonal * field - neighbours(field, padded, weights))
    return field + damping * residue / diagonal


def prolong(values):
    return jnp.repeat(jnp.repeat(jnp.repeat(values, 2, 1), 2, 2), 2, 3)


def cut_span_ends(padded, at_lower, at_upper):
    first = padded[:, :, :1]
    final = padded[:, :, -1:]
    return jnp.concatenate(
        [
            jnp.where(at_lower, jnp.zeros_like(first), first),
            padded[:, :, 1:-1],
            jnp.where(at_upper, jnp.zeros_like(final), final),
        ],
        2,
    )


def shards(grad_rows, dest_rank, dest_block, cell_class, class_stiffness):
    cells_x, cells_y, cells_z = cell_class.shape
    block_count = cells_x * cells_y * cells_z // 128
    span_rank = lax.axis_index("span")
    span_count = lax.axis_size("span")
    slot_cap = 2 * grad_rows.shape[0] // span_count
    at_lower = span_rank == 0
    at_upper = span_rank == span_count - 1
    flat_rows = grad_rows.reshape(grad_rows.shape[0], -1)
    block_ids = jnp.arange(block_count, dtype=jnp.int32)
    rank_list = dest_rank[:, 0]
    chosen = (rank_list[:, None] == jnp.arange(span_count, dtype=jnp.int32)[None, :]).astype(
        jnp.int32
    )
    slot_index = jnp.sum((jnp.cumsum(chosen, 0) - 1) * chosen, axis=1)
    position = rank_list * slot_cap + slot_index
    placed = position[None, :] == jnp.arange(span_count * slot_cap, dtype=jnp.int32)[:, None]
    outgoing = jnp.dot(placed.astype(jnp.float32), flat_rows, precision=lax.Precision.HIGHEST)
    labels = jnp.sum(jnp.where(placed, dest_block[None, :] + 1, 0), axis=1)
    arrived, arrived_labels = (
        lax.all_to_all(outgoing, "span", split_axis=0, concat_axis=0, tiled=True),
        lax.all_to_all(labels, "span", split_axis=0, concat_axis=0, tiled=True),
    )
    wanted = (arrived_labels[None, :] - 1 == block_ids[:, None]).astype(jnp.float32)
    blocks_sum = jnp.dot(wanted, arrived, precision=lax.Precision.HIGHEST)
    source = (
        blocks_sum.reshape(block_count, 3, -1)
        .transpose(1, 0, 2)
        .reshape(3, cells_x, cells_y, cells_z)
    )
    class_pad = extended(cell_class, (("passage", 0), ("span", 1)), 1)
    classes = jnp.arange(class_stiffness.shape[0], dtype=jnp.int32)
    onehot = (classes[:, None, None, None] == class_pad[None]).astype(jnp.float32)
    stiff_pad = jnp.tensordot(class_stiffness, onehot, axes=(0, 0), precision=lax.Precision.HIGHEST)
    stiff_pad = jnp.concatenate(
        [
            jnp.where(at_lower, stiff_pad[:, 1:2], stiff_pad[:, :1]),
            stiff_pad[:, 1:-1],
            jnp.where(at_upper, stiff_pad[:, -2:-1], stiff_pad[:, -1:]),
        ],
        1,
    )
    weights = face_weights(stiff_pad)
    diagonal = diagonal_of(weights)

    def fine_pad(field):
        padded = extended(field, (("passage", 1), ("span", 2)), 1)
        return cut_span_ends(padded, at_lower, at_upper)

    field = damping * source / diagonal
    field = relax_once(field, source, fine_pad(field), weights, diagonal)
    residue = source - (diagonal * field - neighbours(field, fine_pad(field), weights))
    coarse_source = pair_sums(pair_sums(pair_sums(residue, 1), 2), 3)
    coarse_weights = coarsen(weights)
    coarse_diagonal = diagonal_of(coarse_weights)
    correction = damping * coarse_source / coarse_diagonal
    for sweep_count in range(NCOARSE - 1):
        spread_padded = extended(correction, (("passage", 1), ("span", 2)), 1)
        correction = relax_once(
            correction,
            coarse_source,
            cut_span_ends(spread_padded, at_lower, at_upper),
            coarse_weights,
            coarse_diagonal,
        )
    field = field + prolong(correction)
    for sweep_count in range(NPOST):
        field = relax_once(field, source, fine_pad(field), weights, diagonal)
    return field


def solution(mesh):
    placed = (
        P(("passage", "span"), None, None),
        P(("passage", "span"), None),
        P(("passage", "span")),
        P("passage", "span", None),
        P(),
    )
    return jax.shard_map(
        shards,
        mesh=mesh,
        in_specs=placed,
        out_specs=P(None, "passage", "span", None),
        check_vma=False,
    )
```

profile of v0, /device:TPU:1, one launch (start us, length us, event | category | flops | bytes accessed | tf_op | source)
XLA Modules:
  0.0 140.0 jit_solution(15941774968441322008)
XLA Ops:
  4.7 4.3 %all-to-all-start = ((s32[4,256,1]{1,2,0:T(1,128)}), s32[4,256,1]{1,2,0:T(1,128)S(1)}, u32[]{:S(2)}, u32[]{:S(2)}) async-start(s32[4,256,1]{1,2,0:T(1,128)} %bitcast.3), calls=%async_computation | async-start | bytes 8192 | tf_op jit(solution)/shard_map/all_to_all | solution.py:128
  9.7 4.7 %collective-permute-start.1 = (s32[1,16,256]{2,1,0:T(8,128)S(1)}, s32[1,16,256]{2,1,0:T(8,128)S(1)}, u32[]{:S(2)}, u32[]{:S(2)}) collective-permute-start(s32[1,16,256]{2,1,0:T(8,128)S(1)} %get-tuple-element.35), channel_id=1, source_target_pairs={{4,0},{8,4},{12,8},{16,12},{20,16},{24,20},{28,24},{0,28},{5,1},{9... | collective-permute-start | bytes 49160 | tf_op jit(solution)/shard_map/ppermute | solution.py:23
  15.8 3.0 %fusion.2 = f32[4,256,384]{2,1,0:T(8,128)} fusion(f32[512,384,1]{0,1,2:T(8,128)S(1)} %bitcast.79, s32[4,256]{1,0:T(4,128)S(1)} %multiply_add_fusion, s32[512]{0:T(512)S(1)} %get-tuple-element.52), kind=kOutput, calls=%fused_computation.5 | convolution fusion | flops 2416443392 | bytes 2365440 | tf_op jit(solution)/shard_map/dot_general | solution.py:124
  19.8 3.1 %collective-permute-start.2 = (s32[10,1,256]{2,1,0:T(1,128)S(1)}, s32[10,1,256]{2,1,0:T(1,128)S(1)}, u32[]{:S(2)}, u32[]{:S(2)}) collective-permute-start(s32[10,1,256]{2,1,0:T(1,128)S(1)} %get-tuple-element.33), channel_id=1, source_target_pairs={{0,1},{1,2},{2,3},{3,0},{4,5},{5,6},{6,7},{7,4},{8,9},{9,10},{10,1... | collective-permute-start | bytes 30728 | tf_op jit(solution)/shard_map/ppermute | solution.py:20
  22.9 3.7 %all-to-all-start.1 = ((f32[4,256,384]{2,1,0:T(8,128)}), f32[4,256,384]{2,1,0:T(8,128)S(1)}, u32[]{:S(2)}, u32[]{:S(2)}) async-start(f32[4,256,384]{2,1,0:T(8,128)} %fusion.2), calls=%async_computation.1 | async-start | bytes 3145728 | tf_op jit(solution)/shard_map/all_to_all | solution.py:127
  31.3 14.5 %all-to-all-done.1 = f32[4,256,384]{2,1,0:T(8,128)S(1)} async-done(((f32[4,256,384]{2,1,0:T(8,128)}), f32[4,256,384]{2,1,0:T(8,128)S(1)}, u32[]{:S(2)}, u32[]{:S(2)}) %all-to-all-start.1) | async-done | bytes 1572896 | tf_op jit(solution)/shard_map/all_to_all | solution.py:127
  47.8 4.1 %collective-permute-start.5 = (f32[3,1,16,256]{3,2,1,0:T(8,128)S(1)}, f32[3,1,16,256]{3,2,1,0:T(8,128)S(1)}, u32[]{:S(2)}, u32[]{:S(2)}) collective-permute-start(f32[3,1,16,256]{3,2,1,0:T(8,128)S(1)} %get-tuple-element.27), channel_id=1, source_target_pairs={{4,0},{8,4},{12,8},{16,12},{20,16},{24,20},{28,24},{0,28},{5,1},{9... | collective-permute-start | bytes 147464 | tf_op jit(solution)/shard_map/ppermute | solution.py:23
  53.5 2.0 %collective-permute-start.6 = (f32[3,10,1,256]{3,2,1,0:T(1,128)S(1)}, f32[3,10,1,256]{3,2,1,0:T(1,128)S(1)}, u32[]{:S(2)}, u32[]{:S(2)}) collective-permute-start(f32[3,10,1,256]{3,2,1,0:T(1,128)S(1)} %get-tuple-element.18), channel_id=1, source_target_pairs={{0,1},{1,2},{2,3},{3,0},{4,5},{5,6},{6,7},{7,4},{8,9},{9,10},{10,1... | collective-permute-start | bytes 92168 | tf_op jit(solution)/shard_map/ppermute | solution.py:20
  55.7 2.2 %slice.371 = f32[8,16,128]{2,0,1:T(8,128)S(1)} slice(f32[8,16,256]{2,0,1:T(8,128)S(1)} %copy-done.19), slice={[0:8:1], [0:16:1], [0:256:2]} | slice | bytes 131072 | tf_op jit(solution)/shard_map/slice | solution.py:35
  58.0 2.2 %slice.372 = f32[8,16,128]{2,0,1:T(8,128)S(1)} slice(f32[8,16,256]{2,0,1:T(8,128)S(1)} %copy-done.18), slice={[0:8:1], [0:16:1], [1:256:2]} | slice | bytes 131072 | tf_op jit(solution)/shard_map/slice | solution.py:35
  60.9 3.2 %collective-permute-done.7 = f32[3,10,1,256]{3,2,1,0:T(1,128)S(1)} collective-permute-done((f32[3,10,1,256]{3,2,1,0:T(1,128)S(1)}, f32[3,10,1,256]{3,2,1,0:T(1,128)S(1)}, u32[]{:S(2)}, u32[]{:S(2)}) %collective-permute-start.7) | collective-permute-done | bytes 30752 | tf_op jit(solution)/shard_map/ppermute | solution.py:23
  64.7 4.5 %collective-permute-start.9 = (f32[3,1,16,256]{3,2,1,0:T(8,128)S(1)}, f32[3,1,16,256]{3,2,1,0:T(8,128)S(1)}, u32[]{:S(2)}, u32[]{:S(2)}) collective-permute-start(f32[3,1,16,256]{3,2,1,0:T(8,128)S(1)} %get-tuple-element.25), channel_id=1, source_target_pairs={{4,0},{8,4},{12,8},{16,12},{20,16},{24,20},{28,24},{0,28},{5,1},{9... | collective-permute-start | bytes 147464 | tf_op jit(solution)/shard_map/ppermute | solution.py:23
  75.9 2.3 %collective-permute-done.11 = f32[3,10,1,256]{3,2,1,0:T(1,128)S(1)} collective-permute-done((f32[3,10,1,256]{3,2,1,0:T(1,128)S(1)}, f32[3,10,1,256]{3,2,1,0:T(1,128)S(1)}, u32[]{:S(2)}, u32[]{:S(2)}) %collective-permute-start.11) | collective-permute-done | bytes 30752 | tf_op jit(solution)/shard_map/ppermute | solution.py:23
  79.4 2.0 %reduce_sum.184 = f32[3,4,8,128]{2,3,1,0:T(8,128)S(1)} reduce(f32[3,4,8,128,2]{2,4,3,1,0:T(2,128)S(1)} %bitcast.72, f32[]{:T(128)} %constant.31.clone.1), dimensions={4}, to_apply=%region_6.7 | reduce | flops 12288 | bytes 147460 | tf_op jit(solution)/shard_map/reduce_sum | solution.py:31
  81.8 4.1 %collective-permute-start.13 = (f32[3,1,8,128]{3,2,1,0:T(8,128)S(1)}, f32[3,1,8,128]{3,2,1,0:T(8,128)S(1)}, u32[]{:S(2)}, u32[]{:S(2)}) collective-permute-start(f32[3,1,8,128]{3,2,1,0:T(8,128)S(1)} %get-tuple-element.48), channel_id=1, source_target_pairs={{4,0},{8,4},{12,8},{16,12},{20,16},{24,20},{28,24},{0,28},{5,1},{9... | collective-permute-start | bytes 36872 | tf_op jit(solution)/shard_map/ppermute | solution.py:23
  89.0 2.3 %collective-permute-done.15 = f32[3,6,1,128]{3,2,1,0:T(1,128)S(1)} collective-permute-done((f32[3,6,1,128]{3,2,1,0:T(1,128)S(1)}, f32[3,6,1,128]{3,2,1,0:T(1,128)S(1)}, u32[]{:S(2)}, u32[]{:S(2)}) %collective-permute-start.15) | collective-permute-done | bytes 9248 | tf_op jit(solution)/shard_map/ppermute | solution.py:23
  91.5 4.5 %collective-permute-start.17 = (f32[3,1,8,128]{3,2,1,0:T(8,128)S(1)}, f32[3,1,8,128]{3,2,1,0:T(8,128)S(1)}, u32[]{:S(2)}, u32[]{:S(2)}) collective-permute-start(f32[3,1,8,128]{3,2,1,0:T(8,128)S(1)} %get-tuple-element.46), channel_id=1, source_target_pairs={{4,0},{8,4},{12,8},{16,12},{20,16},{24,20},{28,24},{0,28},{5,1},{9... | collective-permute-start | bytes 36872 | tf_op jit(solution)/shard_map/ppermute | solution.py:23
  98.8 2.3 %collective-permute-done.19 = f32[3,6,1,128]{3,2,1,0:T(1,128)S(1)} collective-permute-done((f32[3,6,1,128]{3,2,1,0:T(1,128)S(1)}, f32[3,6,1,128]{3,2,1,0:T(1,128)S(1)}, u32[]{:S(2)}, u32[]{:S(2)}) %collective-permute-start.19) | collective-permute-done | bytes 9248 | tf_op jit(solution)/shard_map/ppermute | solution.py:23
  101.3 4.6 %collective-permute-start.21 = (f32[3,1,8,128]{3,2,1,0:T(8,128)S(1)}, f32[3,1,8,128]{3,2,1,0:T(8,128)S(1)}, u32[]{:S(2)}, u32[]{:S(2)}) collective-permute-start(f32[3,1,8,128]{3,2,1,0:T(8,128)S(1)} %get-tuple-element.44), channel_id=1, source_target_pairs={{4,0},{8,4},{12,8},{16,12},{20,16},{24,20},{28,24},{0,28},{5,1},{9... | collective-permute-start | bytes 36872 | tf_op jit(solution)/shard_map/ppermute | solution.py:23
  108.7 2.3 %collective-permute-done.23 = f32[3,6,1,128]{3,2,1,0:T(1,128)S(1)} collective-permute-done((f32[3,6,1,128]{3,2,1,0:T(1,128)S(1)}, f32[3,6,1,128]{3,2,1,0:T(1,128)S(1)}, u32[]{:S(2)}, u32[]{:S(2)}) %collective-permute-start.23) | collective-permute-done | bytes 9248 | tf_op jit(solution)/shard_map/ppermute | solution.py:23
  117.6 4.6 %collective-permute-start.25 = (f32[3,1,16,256]{3,2,1,0:T(8,128)S(1)}, f32[3,1,16,256]{3,2,1,0:T(8,128)S(1)}, u32[]{:S(2)}, u32[]{:S(2)}) collective-permute-start(f32[3,1,16,256]{3,2,1,0:T(8,128)S(1)} %get-tuple-element.23), channel_id=1, source_target_pairs={{4,0},{8,4},{12,8},{16,12},{20,16},{24,20},{28,24},{0,28},{5,1},{9... | collective-permute-start | bytes 147464 | tf_op jit(solution)/shard_map/ppermute | solution.py:23
  125.6 2.3 %collective-permute-done.27 = f32[3,10,1,256]{3,2,1,0:T(1,128)S(1)} collective-permute-done((f32[3,10,1,256]{3,2,1,0:T(1,128)S(1)}, f32[3,10,1,256]{3,2,1,0:T(1,128)S(1)}, u32[]{:S(2)}, u32[]{:S(2)}) %collective-permute-start.27) | collective-permute-done | bytes 30752 | tf_op jit(solution)/shard_map/ppermute | solution.py:23
  128.5 4.6 %collective-permute-start.29 = (f32[3,1,16,256]{3,2,1,0:T(8,128)S(1)}, f32[3,1,16,256]{3,2,1,0:T(8,128)S(1)}, u32[]{:S(2)}, u32[]{:S(2)}) collective-permute-start(f32[3,1,16,256]{3,2,1,0:T(8,128)S(1)} %get-tuple-element.21), channel_id=1, source_target_pairs={{4,0},{8,4},{12,8},{16,12},{20,16},{24,20},{28,24},{0,28},{5,1},{9... | collective-permute-start | bytes 147464 | tf_op jit(solution)/shard_map/ppermute | solution.py:23
  136.5 2.3 %collective-permute-done.31 = f32[3,10,1,256]{3,2,1,0:T(1,128)S(1)} collective-permute-done((f32[3,10,1,256]{3,2,1,0:T(1,128)S(1)}, f32[3,10,1,256]{3,2,1,0:T(1,128)S(1)}, u32[]{:S(2)}, u32[]{:S(2)}) %collective-permute-start.31) | collective-permute-done | bytes 30752 | tf_op jit(solution)/shard_map/ppermute | solution.py:23
  (220 shorter events, 49.3 us)
Async XLA Ops:
  4.7 18.2 %all-to-all-start = ((s32[4,256,1]{1,2,0:T(1,128)}), s32[4,256,1]{1,2,0:T(1,128)S(1)}, u32[]{:S(2)}, u32[]{:S(2)}) async-start(s32[4,256,1]{1,2,0:T(1,128)} %bitcast.3), calls=%async_computation | async-start | bytes 8192 | tf_op jit(solution)/shard_map/all_to_all | solution.py:128
  9.7 10.0 %collective-permute-start.1 = (s32[1,16,256]{2,1,0:T(8,128)S(1)}, s32[1,16,256]{2,1,0:T(8,128)S(1)}, u32[]{:S(2)}, u32[]{:S(2)}) collective-permute-start(s32[1,16,256]{2,1,0:T(8,128)S(1)} %get-tuple-element.35), channel_id=1, source_target_pairs={{4,0},{8,4},{12,8},{16,12},{20,16},{24,20},{28,24},{0,28},{5,1},{9... | collective-permute-start | bytes 49160 | tf_op jit(solution)/shard_map/ppermute | solution.py:23
  14.4 5.3 %collective-permute-start = (s32[1,16,256]{2,1,0:T(8,128)S(1)}, s32[1,16,256]{2,1,0:T(8,128)S(1)}, u32[]{:S(2)}, u32[]{:S(2)}) collective-permute-start(s32[1,16,256]{2,1,0:T(8,128)S(1)} %get-tuple-element.36), channel_id=1, source_target_pairs={{0,4},{4,8},{8,12},{12,16},{16,20},{20,24},{24,28},{28,0},{1,5},{5... | collective-permute-start | bytes 49160 | tf_op jit(solution)/shard_map/ppermute | solution.py:20
  19.8 6.8 %collective-permute-start.2 = (s32[10,1,256]{2,1,0:T(1,128)S(1)}, s32[10,1,256]{2,1,0:T(1,128)S(1)}, u32[]{:S(2)}, u32[]{:S(2)}) collective-permute-start(s32[10,1,256]{2,1,0:T(1,128)S(1)} %get-tuple-element.33), channel_id=1, source_target_pairs={{0,1},{1,2},{2,3},{3,0},{4,5},{5,6},{6,7},{7,4},{8,9},{9,10},{10,1... | collective-permute-start | bytes 30728 | tf_op jit(solution)/shard_map/ppermute | solution.py:20
  22.9 3.7 %collective-permute-start.3 = (s32[10,1,256]{2,1,0:T(1,128)S(1)}, s32[10,1,256]{2,1,0:T(1,128)S(1)}, u32[]{:S(2)}, u32[]{:S(2)}) collective-permute-start(s32[10,1,256]{2,1,0:T(1,128)S(1)} %get-tuple-element.34), channel_id=1, source_target_pairs={{1,0},{2,1},{3,2},{0,3},{5,4},{6,5},{7,6},{4,7},{9,8},{10,9},{11,1... | collective-permute-start | bytes 30728 | tf_op jit(solution)/shard_map/ppermute | solution.py:23
  22.9 22.9 %all-to-all-start.1 = ((f32[4,256,384]{2,1,0:T(8,128)}), f32[4,256,384]{2,1,0:T(8,128)S(1)}, u32[]{:S(2)}, u32[]{:S(2)}) async-start(f32[4,256,384]{2,1,0:T(8,128)} %fusion.2), calls=%async_computation.1 | async-start | bytes 3145728 | tf_op jit(solution)/shard_map/all_to_all | solution.py:127
  47.8 5.7 %collective-permute-start.4 = (f32[3,1,16,256]{3,2,1,0:T(8,128)S(1)}, f32[3,1,16,256]{3,2,1,0:T(8,128)S(1)}, u32[]{:S(2)}, u32[]{:S(2)}) collective-permute-start(f32[3,1,16,256]{3,2,1,0:T(8,128)S(1)} %get-tuple-element.26), channel_id=1, source_target_pairs={{0,4},{4,8},{8,12},{12,16},{16,20},{20,24},{24,28},{28,0},{1,5},{5... | collective-permute-start | bytes 147464 | tf_op jit(solution)/shard_map/ppermute | solution.py:20
  47.8 5.6 %collective-permute-start.5 = (f32[3,1,16,256]{3,2,1,0:T(8,128)S(1)}, f32[3,1,16,256]{3,2,1,0:T(8,128)S(1)}, u32[]{:S(2)}, u32[]{:S(2)}) collective-permute-start(f32[3,1,16,256]{3,2,1,0:T(8,128)S(1)} %get-tuple-element.27), channel_id=1, source_target_pairs={{4,0},{8,4},{12,8},{16,12},{20,16},{24,20},{28,24},{0,28},{5,1},{9... | collective-permute-start | bytes 147464 | tf_op jit(solution)/shard_map/ppermute | solution.py:23
  53.5 7.4 %collective-permute-start.6 = (f32[3,10,1,256]{3,2,1,0:T(1,128)S(1)}, f32[3,10,1,256]{3,2,1,0:T(1,128)S(1)}, u32[]{:S(2)}, u32[]{:S(2)}) collective-permute-start(f32[3,10,1,256]{3,2,1,0:T(1,128)S(1)} %get-tuple-element.18), channel_id=1, source_target_pairs={{0,1},{1,2},{2,3},{3,0},{4,5},{5,6},{6,7},{7,4},{8,9},{9,10},{10,1... | collective-permute-start | bytes 92168 | tf_op jit(solution)/shard_map/ppermute | solution.py:20
  60.6 3.5 %collective-permute-start.7 = (f32[3,10,1,256]{3,2,1,0:T(1,128)S(1)}, f32[3,10,1,256]{3,2,1,0:T(1,128)S(1)}, u32[]{:S(2)}, u32[]{:S(2)}) collective-permute-start(f32[3,10,1,256]{3,2,1,0:T(1,128)S(1)} %get-tuple-element.19), channel_id=1, source_target_pairs={{1,0},{2,1},{3,2},{0,3},{5,4},{6,5},{7,6},{4,7},{9,8},{10,9},{11,1... | collective-permute-start | bytes 92168 | tf_op jit(solution)/shard_map/ppermute | solution.py:23
  64.6 9.8 %collective-permute-start.8 = (f32[3,1,16,256]{3,2,1,0:T(8,128)S(1)}, f32[3,1,16,256]{3,2,1,0:T(8,128)S(1)}, u32[]{:S(2)}, u32[]{:S(2)}) collective-permute-start(f32[3,1,16,256]{3,2,1,0:T(8,128)S(1)} %get-tuple-element.24), channel_id=1, source_target_pairs={{0,4},{4,8},{8,12},{12,16},{16,20},{20,24},{24,28},{28,0},{1,5},{5... | collective-permute-start | bytes 147464 | tf_op jit(solution)/shard_map/ppermute | solution.py:20
  64.7 9.8 %collective-permute-start.9 = (f32[3,1,16,256]{3,2,1,0:T(8,128)S(1)}, f32[3,1,16,256]{3,2,1,0:T(8,128)S(1)}, u32[]{:S(2)}, u32[]{:S(2)}) collective-permute-start(f32[3,1,16,256]{3,2,1,0:T(8,128)S(1)} %get-tuple-element.25), channel_id=1, source_target_pairs={{4,0},{8,4},{12,8},{16,12},{20,16},{24,20},{28,24},{0,28},{5,1},{9... | collective-permute-start | bytes 147464 | tf_op jit(solution)/shard_map/ppermute | solution.py:23
  74.9 3.4 %collective-permute-start.11 = (f32[3,10,1,256]{3,2,1,0:T(1,128)S(1)}, f32[3,10,1,256]{3,2,1,0:T(1,128)S(1)}, u32[]{:S(2)}, u32[]{:S(2)}) collective-permute-start(f32[3,10,1,256]{3,2,1,0:T(1,128)S(1)} %get-tuple-element.17), channel_id=1, source_target_pairs={{1,0},{2,1},{3,2},{0,3},{5,4},{6,5},{7,6},{4,7},{9,8},{10,9},{11,1... | collective-permute-start | bytes 92168 | tf_op jit(solution)/shard_map/ppermute | solution.py:23
  81.7 5.3 %collective-permute-start.12 = (f32[3,1,8,128]{3,2,1,0:T(8,128)S(1)}, f32[3,1,8,128]{3,2,1,0:T(8,128)S(1)}, u32[]{:S(2)}, u32[]{:S(2)}) collective-permute-start(f32[3,1,8,128]{3,2,1,0:T(8,128)S(1)} %get-tuple-element.47), channel_id=1, source_target_pairs={{0,4},{4,8},{8,12},{12,16},{16,20},{20,24},{24,28},{28,0},{1,5},{5... | collective-permute-start | bytes 36872 | tf_op jit(solution)/shard_map/ppermute | solution.py:20
  81.8 5.2 %collective-permute-start.13 = (f32[3,1,8,128]{3,2,1,0:T(8,128)S(1)}, f32[3,1,8,128]{3,2,1,0:T(8,128)S(1)}, u32[]{:S(2)}, u32[]{:S(2)}) collective-permute-start(f32[3,1,8,128]{3,2,1,0:T(8,128)S(1)} %get-tuple-element.48), channel_id=1, source_target_pairs={{4,0},{8,4},{12,8},{16,12},{20,16},{24,20},{28,24},{0,28},{5,1},{9... | collective-permute-start | bytes 36872 | tf_op jit(solution)/shard_map/ppermute | solution.py:23
  91.5 5.6 %collective-permute-start.16 = (f32[3,1,8,128]{3,2,1,0:T(8,128)S(1)}, f32[3,1,8,128]{3,2,1,0:T(8,128)S(1)}, u32[]{:S(2)}, u32[]{:S(2)}) collective-permute-start(f32[3,1,8,128]{3,2,1,0:T(8,128)S(1)} %get-tuple-element.45), channel_id=1, source_target_pairs={{0,4},{4,8},{8,12},{12,16},{16,20},{20,24},{24,28},{28,0},{1,5},{5... | collective-permute-start | bytes 36872 | tf_op jit(solution)/shard_map/ppermute | solution.py:20
  91.5 5.5 %collective-permute-start.17 = (f32[3,1,8,128]{3,2,1,0:T(8,128)S(1)}, f32[3,1,8,128]{3,2,1,0:T(8,128)S(1)}, u32[]{:S(2)}, u32[]{:S(2)}) collective-permute-start(f32[3,1,8,128]{3,2,1,0:T(8,128)S(1)} %get-tuple-element.46), channel_id=1, source_target_pairs={{4,0},{8,4},{12,8},{16,12},{20,16},{24,20},{28,24},{0,28},{5,1},{9... | collective-permute-start | bytes 36872 | tf_op jit(solution)/shard_map/ppermute | solution.py:23
  101.2 5.6 %collective-permute-start.20 = (f32[3,1,8,128]{3,2,1,0:T(8,128)S(1)}, f32[3,1,8,128]{3,2,1,0:T(8,128)S(1)}, u32[]{:S(2)}, u32[]{:S(2)}) collective-permute-start(f32[3,1,8,128]{3,2,1,0:T(8,128)S(1)} %get-tuple-element.43), channel_id=1, source_target_pairs={{0,4},{4,8},{8,12},{12,16},{16,20},{20,24},{24,28},{28,0},{1,5},{5... | collective-permute-start | bytes 36872 | tf_op jit(solution)/shard_map/ppermute | solution.py:20
  101.3 5.6 %collective-permute-start.21 = (f32[3,1,8,128]{3,2,1,0:T(8,128)S(1)}, f32[3,1,8,128]{3,2,1,0:T(8,128)S(1)}, u32[]{:S(2)}, u32[]{:S(2)}) collective-permute-start(f32[3,1,8,128]{3,2,1,0:T(8,128)S(1)} %get-tuple-element.44), channel_id=1, source_target_pairs={{4,0},{8,4},{12,8},{16,12},{20,16},{24,20},{28,24},{0,28},{5,1},{9... | collective-permute-start | bytes 36872 | tf_op jit(solution)/shard_map/ppermute | solution.py:23
  117.5 6.6 %collective-permute-start.24 = (f32[3,1,16,256]{3,2,1,0:T(8,128)S(1)}, f32[3,1,16,256]{3,2,1,0:T(8,128)S(1)}, u32[]{:S(2)}, u32[]{:S(2)}) collective-permute-start(f32[3,1,16,256]{3,2,1,0:T(8,128)S(1)} %get-tuple-element.22), channel_id=1, source_target_pairs={{0,4},{4,8},{8,12},{12,16},{16,20},{20,24},{24,28},{28,0},{1,5},{5... | collective-permute-start | bytes 147464 | tf_op jit(solution)/shard_map/ppermute | solution.py:20
  117.6 6.5 %collective-permute-start.25 = (f32[3,1,16,256]{3,2,1,0:T(8,128)S(1)}, f32[3,1,16,256]{3,2,1,0:T(8,128)S(1)}, u32[]{:S(2)}, u32[]{:S(2)}) collective-permute-start(f32[3,1,16,256]{3,2,1,0:T(8,128)S(1)} %get-tuple-element.23), channel_id=1, source_target_pairs={{4,0},{8,4},{12,8},{16,12},{20,16},{24,20},{28,24},{0,28},{5,1},{9... | collective-permute-start | bytes 147464 | tf_op jit(solution)/shard_map/ppermute | solution.py:23
  124.6 3.3 %collective-permute-start.27 = (f32[3,10,1,256]{3,2,1,0:T(1,128)S(1)}, f32[3,10,1,256]{3,2,1,0:T(1,128)S(1)}, u32[]{:S(2)}, u32[]{:S(2)}) collective-permute-start(f32[3,10,1,256]{3,2,1,0:T(1,128)S(1)} %get-tuple-element.15), channel_id=1, source_target_pairs={{1,0},{2,1},{3,2},{0,3},{5,4},{6,5},{7,6},{4,7},{9,8},{10,9},{11,1... | collective-permute-start | bytes 92168 | tf_op jit(solution)/shard_map/ppermute | solution.py:23
  128.4 6.5 %collective-permute-start.28 = (f32[3,1,16,256]{3,2,1,0:T(8,128)S(1)}, f32[3,1,16,256]{3,2,1,0:T(8,128)S(1)}, u32[]{:S(2)}, u32[]{:S(2)}) collective-permute-start(f32[3,1,16,256]{3,2,1,0:T(8,128)S(1)} %get-tuple-element.20), channel_id=1, source_target_pairs={{0,4},{4,8},{8,12},{12,16},{16,20},{20,24},{24,28},{28,0},{1,5},{5... | collective-permute-start | bytes 147464 | tf_op jit(solution)/shard_map/ppermute | solution.py:20
  128.5 6.4 %collective-permute-start.29 = (f32[3,1,16,256]{3,2,1,0:T(8,128)S(1)}, f32[3,1,16,256]{3,2,1,0:T(8,128)S(1)}, u32[]{:S(2)}, u32[]{:S(2)}) collective-permute-start(f32[3,1,16,256]{3,2,1,0:T(8,128)S(1)} %get-tuple-element.21), channel_id=1, source_target_pairs={{4,0},{8,4},{12,8},{16,12},{20,16},{24,20},{28,24},{0,28},{5,1},{9... | collective-permute-start | bytes 147464 | tf_op jit(solution)/shard_map/ppermute | solution.py:23
  (38 other events, 394.8 us)
where the time goes:
time: 141 us; the launch traced here: 140 us
  starting transfers between devices  55.2 us (39%)
  waiting for transfers between devices  44.6 us (32%)
  local copies, waits for them, and re-layouts  17.1 us (12%)
  other arithmetic  17.1 us (12%)
  matrix products  5.03 us (4%)
    ppermute x16, starting transfers between devices, extended(): lax.ppermute(lax.slice_in_dim(block, 0, width, axis=dim), axis, backward)  37.3 us
    ppermute x16, waiting for transfers between devices, extended(): lax.ppermute(lax.slice_in_dim(block, 0, width, axis=dim), axis, backward)  17 us
    all_to_all x1, waiting for transfers between devices, shards(): lax.all_to_all(outgoing, 'span', split_axis=0, concat_axis=0, tiled=True)  14.5 us
    ppermute x16, waiting for transfers between devices, extended(): lax.ppermute(lax.slice_in_dim(block, block.shape[dim] - width, None, axis...  13.1 us
    ppermute x16, starting transfers between devices, extended(): lax.ppermute(lax.slice_in_dim(block, block.shape[dim] - width, None, axis...  9.95 us
    reduce_sum x18, other arithmetic, pair_sums(): return values.reshape(new_shape).sum(along + 1)  6.66 us
    slice x6, local copies, waits for them, and re-layouts, every_other(): return lax.slice_in_dim(values, offset, values.shape[along], 2, along)  5.2 us
    all_to_all x1, starting transfers between devices, shards(): lax.all_to_all(labels, 'span', split_axis=0, concat_axis=0, tiled=True)  4.26 us
  transfers between devices with their start and end apart: 34, of which 21 were waited for; matrix products, arithmetic and copies ran while one was open for 14% of the time, Pallas kernels for 0%

commit v1 on v0

v1 whole, which is shorter than its diff:
```python
import functools

import jax
import jax.numpy as jnp
from jax import lax
from jax.experimental import pallas as pl
from jax.experimental.pallas import tpu as pltpu
from jax.sharding import PartitionSpec as P

damping = 0.8
mass_share = 0.02
HALO_S = 7
HALO_F = 3
HALO_C = 4
DIRS = [(dx, dy) for dx in (-1, 0, 1) for dy in (-1, 0, 1) if (dx, dy) != (0, 0)]
MESH = pl.DeviceIdType.MESH


def split2(values):
    high = values.astype(jnp.bfloat16)
    low = (values - high.astype(jnp.float32)).astype(jnp.bfloat16)
    return high, low


def dot(a, b):
    return jnp.dot(a, b, preferred_element_type=jnp.float32)


def as_bf16(mask):
    return jnp.where(mask, 1.0, 0.0).astype(jnp.bfloat16)


def kernel(
    passages, spans, key_ref, rows_ref, class_ref, table_ref, out_ref,
    split_ref, psend, srecv, rsend, rrecv, acc, stiff, fine, fine1, coarse,
    a_ref, d_ref, ca_ref, cd_ref, tmp, tmp2, own_s,
    sib_send, sib_recv, rem_send, rem_recv,
    st_send, st_recv, f_send, f_recv, c_send, c_recv,
):
    nx, ny, nz = class_ref.shape
    half = nz // 2
    blocks = nx * ny * 2
    nrows = rows_ref.shape[1]
    pairs = spans // 2
    p = lax.axis_index("passage")
    s = lax.axis_index("span")
    pair = s // 2
    core = s % 2
    sib = pair * 2 + 1 - core
    at_lower = s == 0
    at_upper = s == spans - 1

    def side(dx):
        return lax.rem(p + dx + passages, passages)

    def inside(dy):
        if dy == 0:
            return None
        return s + dy < spans if dy > 0 else s + dy >= 0

    def guarded(cond, action):
        if cond is None:
            action()
        else:
            pl.when(cond)(action)

    barrier = pltpu.get_barrier_semaphore()
    for dx, dy in DIRS:
        def greet(dx=dx, dy=dy):
            pl.semaphore_signal(barrier, inc=1, device_id=(side(dx), s + dy), device_id_type=MESH)
        guarded(inside(dy), greet)
    pl.semaphore_signal(barrier, inc=1, device_id=(p, sib), device_id_type=MESH)
    for q in range(1, pairs):
        pl.semaphore_signal(
            barrier, inc=1, device_id=(p, lax.rem(pair + q, pairs) * 2 + core), device_id_type=MESH
        )

    def halo(buffer, halo_x, own_x, own_y, send, recv):
        def spans_of(d, width, own, step):
            if d == 0:
                return (width, width, own)
            if d > 0:
                return (own + width - step, 0 + width - step, step)
            return (width, width + own, step)

        copies = []
        for k, (dx, dy) in enumerate(DIRS):
            sx, tx, lx = spans_of(dx, halo_x, own_x, halo_x)
            sy, ty, ly = spans_of(dy, 8, own_y, 8)
            copies.append(
                (dy, pltpu.make_async_remote_copy(
                    src_ref=buffer.at[pl.ds(sx, lx), pl.ds(sy, ly), :],
                    dst_ref=buffer.at[pl.ds(tx, lx), pl.ds(ty, ly), :],
                    send_sem=send.at[k],
                    recv_sem=recv.at[k],
                    device_id=(side(dx), s + dy),
                    device_id_type=MESH,
                ))
            )
        return copies

    def start(copies):
        for dy, copy in copies:
            guarded(inside(dy), copy.start)

    def finish(copies):
        for dy, copy in copies:
            guarded(inside(-dy), copy.wait_recv)
            guarded(inside(dy), copy.wait_send)

    wide_r = lax.broadcasted_iota(jnp.int32, (nz, nz), 0)
    wide_c = lax.broadcasted_iota(jnp.int32, (nz, nz), 1)
    to_halves = as_bf16(wide_r == jnp.where(wide_c < half, 2 * wide_c, 2 * wide_c - (nz - 1)))
    classes = class_ref[...].reshape(nx * ny, nz).astype(jnp.float32).astype(jnp.bfloat16)
    classes = dot(classes, to_halves)
    values = jnp.zeros_like(classes)
    for k in range(table_ref.shape[1]):
        values = jnp.where(classes == float(k), table_ref[0, k], values)
    stiff[pl.ds(HALO_S, nx), pl.ds(8, ny), :] = values.reshape(nx, ny, nz)

    in_r, in_c = wide_r % half, wide_c % half
    rows_perm = as_bf16(
        (wide_r // half == wide_c // half)
        & (in_r == jnp.where(in_c < half // 2, 2 * in_c, 2 * in_c - (half - 1)))
    )
    for c in range(3):
        high, low = split2(rows_ref[c])
        parts = jnp.concatenate([high, low], axis=1)
        split_ref[c] = dot(parts, rows_perm).astype(jnp.bfloat16)

    block_iota = lax.broadcasted_iota(jnp.int32, (blocks, nrows), 0)
    key = key_ref[...]

    def chosen(target):
        return as_bf16(block_iota + target * blocks == key)

    def partial(hot, c):
        both = dot(hot, split_ref[c])
        return both[:, :half] + both[:, half:]

    n_greet = 3 * 2 + 2 + 1 + (pairs - 1)
    missing = 3 * (jnp.where(at_lower, 1, 0) + jnp.where(at_upper, 1, 0))
    pl.semaphore_wait(barrier, n_greet - missing)

    stiff_copies = halo(stiff, HALO_S, nx, ny, st_send, st_recv)
    start(stiff_copies)

    def to_sib(q, c):
        return pltpu.make_async_remote_copy(
            src_ref=psend.at[q, c], dst_ref=srecv.at[q, c],
            send_sem=sib_send.at[q, c], recv_sem=sib_recv.at[q, c],
            device_id=(p, sib), device_id_type=MESH,
        )

    def to_rem(q, c):
        return pltpu.make_async_remote_copy(
            src_ref=rsend.at[q - 1, c], dst_ref=rrecv.at[q - 1, c],
            send_sem=rem_send.at[q - 1, c], recv_sem=rem_recv.at[q - 1, c],
            device_id=(p, lax.rem(pair + q, pairs) * 2 + core), device_id_type=MESH,
        )

    for q in list(range(1, pairs)):
        target = lax.rem(pair + q, pairs) * 2
        hot = chosen(target + 1 - core)
        for c in range(3):
            psend[q, c] = partial(hot, c)
            to_sib(q, c).start()
    for q in range(1, pairs):
        target = lax.rem(pair + q, pairs) * 2
        hot = chosen(target + core)
        for c in range(3):
            own = partial(hot, c)
            to_sib(q, c).wait_recv()
            rsend[q - 1, c] = own + srecv[q, c]
            to_rem(q, c).start()
    hot = chosen(pair * 2 + 1 - core)
    for c in range(3):
        psend[0, c] = partial(hot, c)
        to_sib(0, c).start()
    hot = chosen(s)
    for c in range(3):
        acc[c] = partial(hot, c)

    finish(stiff_copies)
    total_x = nx + 2 * HALO_S

    @pl.when(at_lower)
    def _():
        def body(i, carry):
            stiff[i, pl.ds(0, 8), :] = jnp.broadcast_to(stiff[i, pl.ds(8, 1), :], (8, nz))
            return carry
        lax.fori_loop(0, total_x, body, 0)

    @pl.when(at_upper)
    def _():
        def body(i, carry):
            stiff[i, pl.ds(8 + ny, 8), :] = jnp.broadcast_to(
                stiff[i, pl.ds(7 + ny, 1), :], (8, nz)
            )
            return carry
        lax.fori_loop(0, total_x, body, 0)

    ey = ny + 16
    row_id = lax.broadcasted_iota(jnp.int32, (ey, nz), 0)
    lane_id = lax.broadcasted_iota(jnp.int32, (ey, nz), 1)
    cut_yl = (row_id == 8) & at_lower
    cut_yu = (row_id == 7 + ny) & at_upper
    cut_zl = lane_id == 0
    cut_zu = lane_id == nz - 1

    def up_y(v):
        return pltpu.roll(v, 1, axis=0)

    def down_y(v):
        return pltpu.roll(v, v.shape[0] - 1, axis=0)

    def z_sides(v):
        e, o = v[:, :half], v[:, half:]
        lower = jnp.concatenate([pltpu.roll(o, 1, axis=1), e], axis=1)
        upper = jnp.concatenate([o, pltpu.roll(e, half - 1, axis=1)], axis=1)
        return lower, upper

    def fine_weights(i, carry):
        at = i + HALO_S - 2
        v = stiff[at]
        zl, zu = z_sides(v)
        w = [
            v + stiff[at - 1], v + stiff[at + 1], v + up_y(v), v + down_y(v),
            v + jnp.where(cut_zl, v, zl), v + jnp.where(cut_zu, v, zu),
        ]
        diag = w[0] + w[1] + w[2] + w[3] + w[4] + w[5] + mass_share * v
        inv = damping / diag
        cuts = [None, None, cut_yl, cut_yu, cut_zl, cut_zu]
        for k in range(6):
            a = w[k] * inv
            a_ref[k, i] = a if cuts[k] is None else jnp.where(cuts[k], 0.0, a)
        d_ref[i] = diag
        return carry

    lax.fori_loop(0, nx + 4, fine_weights, 0)

    cy = ey // 2
    ccut_row = lax.broadcasted_iota(jnp.int32, (cy, half), 0)
    ccut_lane = lax.broadcasted_iota(jnp.int32, (cy, half), 1)
    ccut_yl = (ccut_row == 4) & at_lower
    ccut_yu = (ccut_row == 3 + ny // 2) & at_upper
    ccut_zl = ccut_lane == 0
    ccut_zu = ccut_lane == half - 1
    ca_ref[...] = jnp.zeros_like(ca_ref)

    def coarse_weights(i, carry):
        def both(at):
            v = stiff[at]
            return v[:, :half], v[:, half:]
        rows = [both(2 * i + k) for k in range(4)]
        zs = [e + o for e, o in rows]
        even, odd = rows[1][0] + rows[2][0], rows[1][1] + rows[2][1]
        u = even + odd
        for k, v in enumerate([zs[0] + zs[1], zs[2] + zs[3], u, even, odd]):
            tmp[k] = v
        tmp[5] = u + up_y(u)
        tmp[6] = u + down_y(u)

        def lows(k):
            return tmp[k, pl.ds(0, cy, stride=2), :]

        def highs(k):
            return tmp[k, pl.ds(1, cy, stride=2), :]

        def sums(k):
            return lows(k) + highs(k)

        ve, vo = sums(3), sums(4)
        w = [
            sums(0), sums(1), lows(5), highs(6),
            ve + jnp.where(ccut_zl, ve, pltpu.roll(vo, 1, axis=1)),
            vo + jnp.where(ccut_zu, vo, pltpu.roll(ve, half - 1, axis=1)),
        ]
        diag = w[0] + w[1] + w[2] + w[3] + w[4] + w[5] + mass_share * sums(2)
        inv = damping / diag
        cuts = [None, None, ccut_yl, ccut_yu, ccut_zl, ccut_zu]
        for k in range(6):
            a = w[k] * inv
            a = a if cuts[k] is None else jnp.where(cuts[k], 0.0, a)
            ca_ref[k, i, pl.ds(4, cy), :] = a
        cd_ref[i, pl.ds(4, cy), :] = diag
        return carry

    lax.fori_loop(0, nx // 2 + 6, coarse_weights, 0)

    for cond, lo_f, lo_c in ((at_lower, 0, 0), (at_upper, 8 + ny, 8 + ny // 2)):
        @pl.when(cond)
        def _(lo_f=lo_f, lo_c=lo_c):
            def body(i, carry):
                for c in range(3):
                    fine[c, i, pl.ds(lo_f, 8), :] = jnp.zeros((8, nz), jnp.float32)
                return carry
            lax.fori_loop(0, nx + 2 * HALO_F, body, 0)

            def body_c(i, carry):
                for c in range(3):
                    coarse[0, c, i, pl.ds(lo_c, 8), :] = jnp.zeros((8, half), jnp.float32)
                return carry
            lax.fori_loop(0, nx // 2 + 2 * HALO_C, body_c, 0)

    fine_copies = [
        halo(fine.at[c], HALO_F, nx, ny, f_send.at[c], f_recv.at[c]) for c in range(3)
    ]
    coarse_copies = [
        halo(coarse.at[0, c], HALO_C, nx // 2, ny // 2, c_send.at[c], c_recv.at[c])
        for c in range(3)
    ]

    xy = nx * ny
    low_lanes = lax.broadcasted_iota(jnp.int32, (xy, half), 1) < half // 2
    for c in range(3):
        to_sib(0, c).wait_recv()
        total = acc[c] + srecv[0, c]
        for q in range(1, pairs):
            to_rem(q, c).wait_recv()
            total = total + rrecv[q - 1, c]
        first, second = total[:xy], total[xy:]
        even = jnp.where(low_lanes, first, pltpu.roll(second, half // 2, axis=1))
        odd = jnp.where(low_lanes, pltpu.roll(first, half // 2, axis=1), second)
        source = jnp.concatenate([even, odd], axis=1).reshape(nx, ny, nz)
        diag = d_ref[pl.ds(2, nx), pl.ds(8, ny), :]
        fine[c, pl.ds(HALO_F, nx), pl.ds(8, ny), :] = damping * source / diag
        start(fine_copies[c])

    def gathered(ref, at, weights, i):
        v = ref[at]
        zl, zu = z_sides(v)
        return v, (
            weights[0, i] * ref[at - 1] + weights[1, i] * ref[at + 1]
            + weights[2, i] * up_y(v) + weights[3, i] * down_y(v)
            + weights[4, i] * zl + weights[5, i] * zu
        )

    for c in range(3):
        finish(fine_copies[c])
        f0, f1 = fine.at[c], fine1.at[c]

        def second_sweep(i, carry):
            v, near = gathered(f0, i + 1, a_ref, i)
            f1[i] = v * (2.0 - damping) + near
            return carry

        lax.fori_loop(0, nx + 4, second_sweep, 0)

        def restrict(i, carry):
            parts = []
            for k in range(2):
                at = 2 * i + 2 + k
                v, near = gathered(f1, at, a_ref, at)
                parts.append((f0[at + 1] - damping * v + near) * d_ref[at])
            r = parts[0] + parts[1]
            tmp2[...] = r[:, :half] + r[:, half:]
            rc = tmp2[pl.ds(8, ny // 2, stride=2), :] + tmp2[pl.ds(9, ny // 2, stride=2), :]
            coarse[0, c, i + HALO_C, pl.ds(8, ny // 2), :] = (
                rc / cd_ref[i + 3, pl.ds(8, ny // 2), :]
            )
            return carry

        lax.fori_loop(0, nx // 2, restrict, 0)
        start(coarse_copies[c])

    def gathered_c(ref, at, i):
        v = ref[at]
        return v, (
            ca_ref[0, i] * ref[at - 1] + ca_ref[1, i] * ref[at + 1]
            + ca_ref[2, i] * up_y(v) + ca_ref[3, i] * down_y(v)
            + ca_ref[4, i] * pltpu.roll(v, 1, axis=1)
            + ca_ref[5, i] * pltpu.roll(v, half - 1, axis=1)
        )

    from_halves = as_bf16(wide_c == jnp.where(wide_r < half, 2 * wide_r, 2 * wide_r - (nz - 1)))
    cx = nx // 2
    for c in range(3):
        finish(coarse_copies[c])
        c1 = coarse.at[0, c]
        for sweep in range(3):
            old, new = coarse.at[sweep, c], coarse.at[sweep + 1, c]

            def coarse_sweep(i, carry):
                v, near = gathered_c(old, i + 1, i)
                new[i + 1] = c1[i + 1] + (1.0 - damping) * v + near
                return carry

            lax.fori_loop(sweep, cx + 6 - sweep, coarse_sweep, 0)
        c4 = coarse.at[3, c]
        f0, f1 = fine.at[c], fine1.at[c]

        def prolong(i, carry):
            v = c4[i + 3, pl.ds(4, cy), :]
            tmp2[pl.ds(0, cy, stride=2), :] = v
            tmp2[pl.ds(1, cy, stride=2), :] = v
            w = tmp2[...]
            w = jnp.concatenate([w, w], axis=1)
            f1[2 * i] = f1[2 * i] + w
            f1[2 * i + 1] = f1[2 * i + 1] + w
            return carry

        lax.fori_loop(0, cx + 2, prolong, 0)

        def post1(i, carry):
            v, near = gathered(f1, i + 1, a_ref, i + 1)
            own_s[i] = f0[i + 2] + (1.0 - damping) * v + near
            return carry

        lax.fori_loop(0, nx + 2, post1, 0)

        def post2(i, carry):
            v, near = gathered(own_s, i + 1, a_ref, i + 2)
            r = (f0[i + 3] + (1.0 - damping) * v + near)[8:8 + ny]
            high, low = split2(r)
            out_ref[c, i] = dot(high, from_halves) + dot(low, from_halves)
            return carry

        lax.fori_loop(0, nx, post2, 0)

    for c in range(3):
        for q in range(pairs):
            to_sib(q, c).wait_send()
        for q in range(1, pairs):
            to_rem(q, c).wait_send()


def shards(mesh, grad_rows, dest_rank, dest_block, cell_class, class_stiffness):
    nx, ny, nz = cell_class.shape
    half = nz // 2
    passages, spans = mesh.shape["passage"], mesh.shape["span"]
    pairs = spans // 2
    nrows = grad_rows.shape[0]
    blocks = nx * ny * 2
    key = dest_rank[:, 0] * blocks + (dest_block % 2) * (blocks // 2) + dest_block // 2
    rows = grad_rows.transpose(1, 0, 2)
    vmem = pl.BlockSpec(memory_space=pltpu.VMEM)
    f32 = jnp.float32
    ey = ny + 16
    cx, ecy = nx // 2, ny // 2 + 16
    return pl.pallas_call(
        functools.partial(kernel, passages, spans),
        out_shape=jax.ShapeDtypeStruct((3, nx, ny, nz), f32),
        in_specs=[vmem, vmem, vmem, pl.BlockSpec(memory_space=pltpu.SMEM)],
        out_specs=vmem,
        scratch_shapes=[
            pltpu.VMEM((3, nrows, nz), jnp.bfloat16),
            pltpu.VMEM((pairs, 3, blocks, half), f32),
            pltpu.VMEM((pairs, 3, blocks, half), f32),
            pltpu.VMEM((pairs - 1, 3, blocks, half), f32),
            pltpu.VMEM((pairs - 1, 3, blocks, half), f32),
            pltpu.VMEM((3, blocks, half), f32),
            pltpu.VMEM((nx + 2 * HALO_S, ey, nz), f32),
            pltpu.VMEM((3, nx + 2 * HALO_F, ey, nz), f32),
            pltpu.VMEM((3, nx + 4, ey, nz), f32),
            pltpu.VMEM((4, 3, cx + 2 * HALO_C, ecy, half), f32),
            pltpu.VMEM((6, nx + 4, ey, nz), f32),
            pltpu.VMEM((nx + 4, ey, nz), f32),
            pltpu.VMEM((6, cx + 6, ecy, half), f32),
            pltpu.VMEM((cx + 6, ecy, half), f32),
            pltpu.VMEM((7, ey, half), f32),
            pltpu.VMEM((ey, half), f32),
            pltpu.VMEM((nx + 2, ey, nz), f32),
            pltpu.SemaphoreType.DMA((pairs, 3)),
            pltpu.SemaphoreType.DMA((pairs, 3)),
            pltpu.SemaphoreType.DMA((pairs - 1, 3)),
            pltpu.SemaphoreType.DMA((pairs - 1, 3)),
            pltpu.SemaphoreType.DMA((8,)),
            pltpu.SemaphoreType.DMA((8,)),
            pltpu.SemaphoreType.DMA((3, 8)),
            pltpu.SemaphoreType.DMA((3, 8)),
            pltpu.SemaphoreType.DMA((3, 8)),
            pltpu.SemaphoreType.DMA((3, 8)),
        ],
        compiler_params=pltpu.CompilerParams(
            collective_id=0, has_side_effects=True, vmem_limit_bytes=48 * 1024 * 1024
        ),
    )(key[None, :], rows, cell_class, class_stiffness[None, :])


def solution(mesh):
    placed = (
        P(("passage", "span"), None, None),
        P(("passage", "span"), None),
        P(("passage", "span")),
        P("passage", "span", None),
        P(),
    )
    return jax.shard_map(
        functools.partial(shards, mesh),
        mesh=mesh,
        in_specs=placed,
        out_specs=P(None, "passage", "span", None),
        check_vma=False,
    )
```

time: 141 us -> 53.2 us (0.38)
  starting transfers between devices: 55.2 us -> 0 us
  Pallas kernels: 0 us -> 47.8 us
  waiting for transfers between devices: 44.6 us -> 0 us
  other arithmetic: 17.1 us -> 0.02 us
  local copies, waits for them, and re-layouts: 17.1 us -> 4.79 us
  matrix products: 5.03 us -> 0 us
    pallas_call x0 -> x1, Pallas kernels: none -> 47.8 us  [shards(): pl.pallas_call(functools.partial(kernel, passages, spans), out_shape=jax....]
    ppermute x32 -> x0, starting transfers between devices: 47.2 us -> none  [the longest x16 37.3 us: extended(): lax.ppermute(lax.slice_in_dim(block, 0, width, axis=dim), axis, backward)]
    ppermute x32 -> x0, waiting for transfers between devices: 30 us -> none  [the longest x16 17 us: extended(): lax.ppermute(lax.slice_in_dim(block, 0, width, axis=dim), axis, backward)]
    all_to_all x2 -> x0, waiting for transfers between devices: 14.5 us -> none  [the longest x1 14.5 us: shards(): lax.all_to_all(outgoing, 'span', split_axis=0, concat_axis=0, tiled=True)]
    reduce_sum x20 -> x0, other arithmetic: 8.25 us -> none  [the longest x18 6.66 us: pair_sums(): return values.reshape(new_shape).sum(along + 1)]
    all_to_all x2 -> x0, starting transfers between devices: 7.94 us -> none  [the longest x1 4.26 us: shards(): lax.all_to_all(labels, 'span', split_axis=0, concat_axis=0, tiled=True)]
    slice x18 -> x0, local copies, waits for them, and re-layouts: 6.13 us -> none  [the longest x6 5.2 us: every_other(): return lax.slice_in_dim(values, offset, values.shape[along], 2, along)]
    add x9 -> x1, other arithmetic: 5.15 us -> 0.01 us  [shards(): dest_rank[:, 0] * blocks + dest_block % 2 * (blocks // 2) + dest_block // 2]
  transfers between devices with their start and end apart: 34 -> 0, of which waited for: 21 -> 0; matrix products, arithmetic and copies ran while one was open for 14% -> 0% of each run, Pallas kernels for 0% -> 0%
where the time goes in v1:
time: 53.2 us; the launch traced here: 52.7 us
  Pallas kernels  47.8 us (90%)
  local copies, waits for them, and re-layouts  4.79 us (9%)
    pallas_call x1, Pallas kernels, shards(): pl.pallas_call(functools.partial(kernel, passages, spans), out_shape=jax....  47.8 us
    unnamed x11, local copies, waits for them, and re-layouts  4.79 us

profile of v1, /device:TPU:1, one launch (start us, length us, event | category | flops | bytes accessed | tf_op | source)
XLA Modules:
  0.0 52.7 jit_solution(14261818614354943506)
XLA Ops:
  0.0 0.0 copy-start.4
  0.0 0.7 %copy-done.4 = s32[512,1]{0,1:T(1,128)S(1)} copy-done((s32[512,1]{0,1:T(1,128)S(1)}, s32[512,1]{0,1:T(1,128)}, u32[]{:S(2)}) %copy-start.4) | copy-done | bytes 2072
  0.7 0.0 copy-start.3
  0.7 0.7 %copy-done.3 = s32[512]{0:T(512)S(1)} copy-done((s32[512]{0:T(512)S(1)}, s32[512]{0:T(512)}, u32[]{:S(2)}) %copy-start.3) | copy-done | bytes 2072
  1.4 0.0 copy-start.2
  1.4 0.6 %copy-done.2 = f32[16]{0:T(128)S(1)} copy-done((f32[16]{0:T(128)S(1)}, f32[16]{0:T(128)}, u32[]{:S(2)}) %copy-start.2) | copy-done | bytes 88
  2.0 0.0 copy-start
  2.0 1.1 %copy-done = f32[512,3,128]{2,0,1:T(8,128)S(1)} copy-done((f32[512,3,128]{2,0,1:T(8,128)S(1)}, f32[512,3,128]{2,0,1:T(8,128)}, u32[]{:S(2)}) %copy-start) | copy-done | bytes 786456
  3.2 0.0 copy-start.1
  3.2 0.9 %copy-done.1 = s32[8,16,256]{2,1,0:T(8,128)S(1)} copy-done((s32[8,16,256]{2,1,0:T(8,128)S(1)}, s32[8,16,256]{2,1,0:T(8,128)}, u32[]{:S(2)}) %copy-start.1) | copy-done | bytes 131096
  4.1 47.8 %shard_map.55 = f32[3,8,16,256]{3,2,1,0:T(8,128)S(1)} custom-call(s32[1,512]{1,0:T(1,128)S(1)} %bitcast.5, f32[3,512,128]{2,1,0:T(8,128)S(1)} %bitcast.4, s32[8,16,256]{2,1,0:T(8,128)S(1)} %copy-done.1, f32[1,16]{1,0:T(1,128)S(1)} %bitcast.6), custom_call_target="tpu_custom_call" | custom-call | tf_op jit(solution)/shard_map/pallas_call | solution.py:441
  51.9 0.7 %copy.7 = f32[3,8,16,256]{3,2,1,0:T(8,128)} copy(f32[3,8,16,256]{3,2,1,0:T(8,128)S(1)} %shard_map.55) | data formatting | bytes 786432
  (2 shorter events, 0.0 us)
Async XLA Ops:
  0.0 0.7 %copy-start.4 = (s32[512,1]{0,1:T(1,128)S(1)}, s32[512,1]{0,1:T(1,128)}, u32[]{:S(2)}) copy-start(s32[512,1]{0,1:T(1,128)} %param.6) | copy-start | bytes 6148
  0.7 0.7 %copy-start.3 = (s32[512]{0:T(512)S(1)}, s32[512]{0:T(512)}, u32[]{:S(2)}) copy-start(s32[512]{0:T(512)} %param.7) | copy-start | bytes 6148
  1.4 0.7 %copy-start.2 = (f32[16]{0:T(128)S(1)}, f32[16]{0:T(128)}, u32[]{:S(2)}) copy-start(f32[16]{0:T(128)} %param.9) | copy-start | bytes 196
  2.0 1.1 %copy-start = (f32[512,3,128]{2,0,1:T(8,128)S(1)}, f32[512,3,128]{2,0,1:T(8,128)}, u32[]{:S(2)}) copy-start(f32[512,3,128]{2,0,1:T(8,128)} %param.5) | copy-start | bytes 2359300
  3.2 0.9 %copy-start.1 = (s32[8,16,256]{2,1,0:T(8,128)S(1)}, s32[8,16,256]{2,1,0:T(8,128)}, u32[]{:S(2)}) copy-start(s32[8,16,256]{2,1,0:T(8,128)} %class_ref.1) | copy-start | bytes 393220

commit v2 on v1

--- a/solution.py
+++ b/solution.py
@@ -26,12 +26,18 @@
     return jnp.dot(a, b, preferred_element_type=jnp.float32)
 
 
+def unrolled(low, high, body):
+    for i in range(low, high):
+        body(i, 0)
+
+
 def as_bf16(mask):
     return jnp.where(mask, 1.0, 0.0).astype(jnp.bfloat16)
 
 
 def kernel(
-    passages, spans, key_ref, rows_ref, class_ref, table_ref, out_ref,
+    passages, spans, key_hbm, rows_hbm, class_hbm, table_ref, out_ref,
+    key_ref, rows_ref, class_ref, in_sem,
     split_ref, psend, srecv, rsend, rrecv, acc, stiff, fine, fine1, coarse,
     a_ref, d_ref, ca_ref, cd_ref, tmp, tmp2, own_s,
     sib_send, sib_recv, rem_send, rem_recv,
@@ -75,17 +81,27 @@
             barrier, inc=1, device_id=(p, lax.rem(pair + q, pairs) * 2 + core), device_id_type=MESH
         )
 
-    def halo(buffer, halo_x, own_x, own_y, send, recv):
+    class_copy = pltpu.make_async_copy(class_hbm, class_ref, in_sem.at[0])
+    class_copy.start()
+    rows_copies = [
+        pltpu.make_async_copy(rows_hbm.at[c], rows_ref.at[c], in_sem.at[1 + c]) for c in range(3)
+    ]
+    for copy in rows_copies:
+        copy.start()
+    key_copy = pltpu.make_async_copy(key_hbm, key_ref, in_sem.at[4])
+    key_copy.start()
+
+    def halo(buffer, halo_x, own_x, own_y, corner, send, recv):
         def spans_of(d, width, own, step):
             if d == 0:
                 return (width, width, own)
             if d > 0:
-                return (own + width - step, 0 + width - step, step)
+                return (own + width - step, width - step, step)
             return (width, width + own, step)
 
         copies = []
         for k, (dx, dy) in enumerate(DIRS):
-            sx, tx, lx = spans_of(dx, halo_x, own_x, halo_x)
+            sx, tx, lx = spans_of(dx, halo_x, own_x, halo_x if dy == 0 else corner)
             sy, ty, ly = spans_of(dy, 8, own_y, 8)
             copies.append(
                 (dy, pltpu.make_async_remote_copy(
@@ -111,6 +127,7 @@
     wide_r = lax.broadcasted_iota(jnp.int32, (nz, nz), 0)
     wide_c = lax.broadcasted_iota(jnp.int32, (nz, nz), 1)
     to_halves = as_bf16(wide_r == jnp.where(wide_c < half, 2 * wide_c, 2 * wide_c - (nz - 1)))
+    class_copy.wait()
     classes = class_ref[...].reshape(nx * ny, nz).astype(jnp.float32).astype(jnp.bfloat16)
     classes = dot(classes, to_halves)
     values = jnp.zeros_like(classes)
@@ -124,11 +141,13 @@
         & (in_r == jnp.where(in_c < half // 2, 2 * in_c, 2 * in_c - (half - 1)))
     )
     for c in range(3):
+        rows_copies[c].wait()
         high, low = split2(rows_ref[c])
         parts = jnp.concatenate([high, low], axis=1)
         split_ref[c] = dot(parts, rows_perm).astype(jnp.bfloat16)
 
     block_iota = lax.broadcasted_iota(jnp.int32, (blocks, nrows), 0)
+    key_copy.wait()
     key = key_ref[...]
 
     def chosen(target):
@@ -142,7 +161,7 @@
     missing = 3 * (jnp.where(at_lower, 1, 0) + jnp.where(at_upper, 1, 0))
     pl.semaphore_wait(barrier, n_greet - missing)
 
-    stiff_copies = halo(stiff, HALO_S, nx, ny, st_send, st_recv)
+    stiff_copies = halo(stiff, HALO_S, nx, ny, HALO_S, st_send, st_recv)
     start(stiff_copies)
 
     def to_sib(q, c):
@@ -237,7 +256,7 @@
         d_ref[i] = diag
         return carry
 
-    lax.fori_loop(0, nx + 4, fine_weights, 0)
+    lax.fori_loop(0, nx + 4, fine_weights, 0, unroll=2)
 
     cy = ey // 2
     ccut_row = lax.broadcasted_iota(jnp.int32, (cy, half), 0)
@@ -286,7 +305,7 @@
         cd_ref[i, pl.ds(4, cy), :] = diag
         return carry
 
-    lax.fori_loop(0, nx // 2 + 6, coarse_weights, 0)
+    lax.fori_loop(0, nx // 2 + 6, coarse_weights, 0, unroll=2)
 
     for cond, lo_f, lo_c in ((at_lower, 0, 0), (at_upper, 8 + ny, 8 + ny // 2)):
         @pl.when(cond)
@@ -303,11 +322,16 @@
                 return carry
             lax.fori_loop(0, nx // 2 + 2 * HALO_C, body_c, 0)
 
+    for c in range(3):
+        for at in (0, nx + 2 * HALO_F - 1):
+            for lo in (0, 8 + ny):
+                fine[c, at, pl.ds(lo, 8), :] = jnp.zeros((8, nz), jnp.float32)
+
     fine_copies = [
-        halo(fine.at[c], HALO_F, nx, ny, f_send.at[c], f_recv.at[c]) for c in range(3)
+        halo(fine.at[c], HALO_F, nx, ny, HALO_F - 1, f_send.at[c], f_recv.at[c]) for c in range(3)
     ]
     coarse_copies = [
-        halo(coarse.at[0, c], HALO_C, nx // 2, ny // 2, c_send.at[c], c_recv.at[c])
+        halo(coarse.at[0, c], HALO_C, nx // 2, ny // 2, HALO_C, c_send.at[c], c_recv.at[c])
         for c in range(3)
     ]
 
@@ -345,7 +369,7 @@
             f1[i] = v * (2.0 - damping) + near
             return carry
 
-        lax.fori_loop(0, nx + 4, second_sweep, 0)
+        unrolled(0, nx + 4, second_sweep)
 
         def restrict(i, carry):
             parts = []
@@ -354,14 +378,15 @@
                 v, near = gathered(f1, at, a_ref, at)
                 parts.append((f0[at + 1] - damping * v + near) * d_ref[at])
             r = parts[0] + parts[1]
-            tmp2[...] = r[:, :half] + r[:, half:]
+            r = r[8:8 + ny]
+            tmp2[pl.ds(8, ny), :] = r[:, :half] + r[:, half:]
             rc = tmp2[pl.ds(8, ny // 2, stride=2), :] + tmp2[pl.ds(9, ny // 2, stride=2), :]
             coarse[0, c, i + HALO_C, pl.ds(8, ny // 2), :] = (
                 rc / cd_ref[i + 3, pl.ds(8, ny // 2), :]
             )
             return carry
 
-        lax.fori_loop(0, nx // 2, restrict, 0)
+        unrolled(0, nx // 2, restrict)
         start(coarse_copies[c])
 
     def gathered_c(ref, at, i):
@@ -386,7 +411,7 @@
                 new[i + 1] = c1[i + 1] + (1.0 - damping) * v + near
                 return carry
 
-            lax.fori_loop(sweep, cx + 6 - sweep, coarse_sweep, 0)
+            unrolled(sweep, cx + 6 - sweep, coarse_sweep)
         c4 = coarse.at[3, c]
         f0, f1 = fine.at[c], fine1.at[c]
 
@@ -400,14 +425,14 @@
             f1[2 * i + 1] = f1[2 * i + 1] + w
             return carry
 
-        lax.fori_loop(0, cx + 2, prolong, 0)
+        unrolled(0, cx + 2, prolong)
 
         def post1(i, carry):
             v, near = gathered(f1, i + 1, a_ref, i + 1)
             own_s[i] = f0[i + 2] + (1.0 - damping) * v + near
             return carry
 
-        lax.fori_loop(0, nx + 2, post1, 0)
+        unrolled(0, nx + 2, post1)
 
         def post2(i, carry):
             v, near = gathered(own_s, i + 1, a_ref, i + 2)
@@ -416,7 +441,7 @@
             out_ref[c, i] = dot(high, from_halves) + dot(low, from_halves)
             return carry
 
-        lax.fori_loop(0, nx, post2, 0)
+        unrolled(0, nx, post2)
 
     for c in range(3):
         for q in range(pairs):
@@ -435,15 +460,20 @@
     key = dest_rank[:, 0] * blocks + (dest_block % 2) * (blocks // 2) + dest_block // 2
     rows = grad_rows.transpose(1, 0, 2)
     vmem = pl.BlockSpec(memory_space=pltpu.VMEM)
+    hbm = pl.BlockSpec(memory_space=pl.ANY)
     f32 = jnp.float32
     ey = ny + 16
     cx, ecy = nx // 2, ny // 2 + 16
     return pl.pallas_call(
         functools.partial(kernel, passages, spans),
         out_shape=jax.ShapeDtypeStruct((3, nx, ny, nz), f32),
-        in_specs=[vmem, vmem, vmem, pl.BlockSpec(memory_space=pltpu.SMEM)],
+        in_specs=[hbm, hbm, hbm, pl.BlockSpec(memory_space=pltpu.SMEM)],
         out_specs=vmem,
         scratch_shapes=[
+            pltpu.VMEM((1, nrows), jnp.int32),
+            pltpu.VMEM((3, nrows, half), f32),
+            pltpu.VMEM((nx, ny, nz), jnp.int32),
+            pltpu.SemaphoreType.DMA((5,)),
             pltpu.VMEM((3, nrows, nz), jnp.bfloat16),
             pltpu.VMEM((pairs, 3, blocks, half), f32),
             pltpu.VMEM((pairs, 3, blocks, half), f32),
@@ -473,7 +503,7 @@
             pltpu.SemaphoreType.DMA((3, 8)),
         ],
         compiler_params=pltpu.CompilerParams(
-            collective_id=0, has_side_effects=True, vmem_limit_bytes=48 * 1024 * 1024
+            collective_id=0, has_side_effects=True, vmem_limit_bytes=60 * 1024 * 1024
         ),
     )(key[None, :], rows, cell_class, class_stiffness[None, :])
 

time: 53.2 us -> 42.3 us (0.80)
  Pallas kernels: 47.8 us -> 37.9 us
  local copies, waits for them, and re-layouts: 4.79 us -> 3.13 us
  other arithmetic: 0.02 us -> 0.59 us
    pallas_call x1, Pallas kernels: 47.8 us -> 37.9 us  [shards(): pl.pallas_call(functools.partial(kernel, passages, spans), out_shape=jax....]
    unnamed x11 -> x5, local copies, waits for them, and re-layouts: 4.79 us -> 3.13 us
    add x1, other arithmetic: 0.01 us -> 0.59 us  [shards(): dest_rank[:, 0] * blocks + dest_block % 2 * (blocks // 2) + dest_block // 2]
where the time goes in v2:
time: 42.3 us; the launch traced here: 41.7 us
  Pallas kernels  37.9 us (90%)
  local copies, waits for them, and re-layouts  3.13 us (7%)
  other arithmetic  0.59 us (1%)
    pallas_call x1, Pallas kernels, shards(): pl.pallas_call(functools.partial(kernel, passages, spans), out_shape=jax....  37.9 us
    unnamed x5, local copies, waits for them, and re-layouts  3.13 us

profile of v2, /device:TPU:1, one launch (start us, length us, event | category | flops | bytes accessed | tf_op | source)
XLA Modules:
  0.0 41.7 jit_solution(6068290242549075333)
XLA Ops:
  0.0 0.0 copy-start.1
  0.0 0.7 %copy-done.1 = s32[512,1]{0,1:T(1,128)S(1)} copy-done((s32[512,1]{0,1:T(1,128)S(1)}, s32[512,1]{0,1:T(1,128)}, u32[]{:S(2)}) %copy-start.1) | copy-done | bytes 2072
  0.7 0.0 copy-start
  0.7 0.7 %copy-done = s32[512]{0:T(512)S(1)} copy-done((s32[512]{0:T(512)S(1)}, s32[512]{0:T(512)}, u32[]{:S(2)}) %copy-start) | copy-done | bytes 2072
  1.4 0.6 %fusion.2 = s32[512]{0:T(512)} fusion(s32[512]{0:T(512)S(1)} %bitcast.6, s32[512]{0:T(512)S(1)} %copy-done), kind=kLoop, calls=%fused_computation.7 | loop fusion | flops 11264 | bytes 6144 | tf_op jit(solution)/shard_map/add | solution.py:460
  2.0 37.9 %shard_map.55 = f32[3,8,16,256]{3,2,1,0:T(8,128)} custom-call(s32[1,512]{1,0:T(1,128)} %bitcast.5, f32[3,512,128]{2,1,0:T(8,128)} %bitcast.4, s32[8,16,256]{2,1,0:T(8,128)} %class_hbm.1, f32[1,16]{1,0:T(1,128)} %bitcast.7), custom_call_target="tpu_custom_call" | custom-call | tf_op jit(solution)/shard_map/pallas_call | solution.py:467
  39.9 1.8 %copy.7 = f32[3,8,16,256]{3,2,1,0:T(8,128)} copy(f32[3,8,16,256]{3,2,1,0:T(8,128)} %shard_map.55) | data formatting | bytes 786432
  (1 shorter events, 0.0 us)
Async XLA Ops:
  0.0 0.7 %copy-start.1 = (s32[512,1]{0,1:T(1,128)S(1)}, s32[512,1]{0,1:T(1,128)}, u32[]{:S(2)}) copy-start(s32[512,1]{0,1:T(1,128)} %param.6) | copy-start | bytes 6148
  0.7 0.7 %copy-start = (s32[512]{0:T(512)S(1)}, s32[512]{0:T(512)}, u32[]{:S(2)}) copy-start(s32[512]{0:T(512)} %param.7) | copy-start | bytes 6148

commit v3 on v2

--- a/solution.py
+++ b/solution.py
@@ -12,7 +12,8 @@
 HALO_S = 7
 HALO_F = 3
 HALO_C = 4
-DIRS = [(dx, dy) for dx in (-1, 0, 1) for dy in (-1, 0, 1) if (dx, dy) != (0, 0)]
+DIRS = [(-1, 0), (1, 0), (0, -1), (0, 1)]
+CORNERS = [(dx, dy) for dx in (-1, 1) for dy in (-1, 1)]
 MESH = pl.DeviceIdType.MESH
 
 
@@ -39,7 +40,7 @@
     passages, spans, key_hbm, rows_hbm, class_hbm, table_ref, out_ref,
     key_ref, rows_ref, class_ref, in_sem,
     split_ref, psend, srecv, rsend, rrecv, acc, stiff, fine, fine1, coarse,
-    a_ref, d_ref, ca_ref, cd_ref, tmp, tmp2, own_s,
+    inv_d, a_ref, d_ref, ca_ref, cd_ref, tmp, tmp2, own_s,
     sib_send, sib_recv, rem_send, rem_recv,
     st_send, st_recv, f_send, f_recv, c_send, c_recv,
 ):
@@ -92,36 +93,42 @@
     key_copy.start()
 
     def halo(buffer, halo_x, own_x, own_y, corner, send, recv):
-        def spans_of(d, width, own, step):
-            if d == 0:
-                return (width, width, own)
-            if d > 0:
-                return (own + width - step, width - step, step)
-            return (width, width + own, step)
-
-        copies = []
+        def copy(k, target, sx, tx, lx, sy, ty, ly):
+            return pltpu.make_async_remote_copy(
+                src_ref=buffer.at[pl.ds(sx, lx), pl.ds(sy, ly), :],
+                dst_ref=buffer.at[pl.ds(tx, lx), pl.ds(ty, ly), :],
+                send_sem=send.at[k],
+                recv_sem=recv.at[k],
+                device_id=target,
+                device_id_type=MESH,
+            )
+
+        def along_y(dy):
+            return (own_y, 0, 8) if dy > 0 else (8, 8 + own_y, 8)
+
+        first, second = [], []
         for k, (dx, dy) in enumerate(DIRS):
-            sx, tx, lx = spans_of(dx, halo_x, own_x, halo_x if dy == 0 else corner)
-            sy, ty, ly = spans_of(dy, 8, own_y, 8)
-            copies.append(
-                (dy, pltpu.make_async_remote_copy(
-                    src_ref=buffer.at[pl.ds(sx, lx), pl.ds(sy, ly), :],
-                    dst_ref=buffer.at[pl.ds(tx, lx), pl.ds(ty, ly), :],
-                    send_sem=send.at[k],
-                    recv_sem=recv.at[k],
-                    device_id=(side(dx), s + dy),
-                    device_id_type=MESH,
-                ))
-            )
-        return copies
+            if dx:
+                strip = (own_x, 0, halo_x) if dx > 0 else (halo_x, halo_x + own_x, halo_x)
+                rows = (8, 8, own_y)
+            else:
+                strip, rows = (halo_x, halo_x, own_x), along_y(dy)
+            first.append((dy, copy(k, (side(dx), s + dy), *strip, *rows)))
+        for k, (dx, dy) in enumerate(CORNERS):
+            at = halo_x - corner if dx < 0 else halo_x + own_x
+            second.append((dy, copy(4 + k, (p, s + dy), at, at, corner, *along_y(dy))))
+        return first, second
 
     def start(copies):
         for dy, copy in copies:
             guarded(inside(dy), copy.start)
 
-    def finish(copies):
+    def arrive(copies):
         for dy, copy in copies:
             guarded(inside(-dy), copy.wait_recv)
+
+    def sent(copies):
+        for dy, copy in copies:
             guarded(inside(dy), copy.wait_send)
 
     wide_r = lax.broadcasted_iota(jnp.int32, (nz, nz), 0)
@@ -157,12 +164,12 @@
         both = dot(hot, split_ref[c])
         return both[:, :half] + both[:, half:]
 
-    n_greet = 3 * 2 + 2 + 1 + (pairs - 1)
-    missing = 3 * (jnp.where(at_lower, 1, 0) + jnp.where(at_upper, 1, 0))
+    n_greet = 2 + 2 + 1 + (pairs - 1)
+    missing = (jnp.where(at_lower, 1, 0) + jnp.where(at_upper, 1, 0))
     pl.semaphore_wait(barrier, n_greet - missing)
 
-    stiff_copies = halo(stiff, HALO_S, nx, ny, HALO_S, st_send, st_recv)
-    start(stiff_copies)
+    stiff_first, stiff_second = halo(stiff, HALO_S, nx, ny, HALO_S, st_send, st_recv)
+    start(stiff_first)
 
     def to_sib(q, c):
         return pltpu.make_async_remote_copy(
@@ -200,7 +207,8 @@
     for c in range(3):
         acc[c] = partial(hot, c)
 
-    finish(stiff_copies)
+    arrive(stiff_first)
+    start(stiff_second)
     total_x = nx + 2 * HALO_S
 
     @pl.when(at_lower)
@@ -238,6 +246,20 @@
         lower = jnp.concatenate([pltpu.roll(o, 1, axis=1), e], axis=1)
         upper = jnp.concatenate([o, pltpu.roll(e, half - 1, axis=1)], axis=1)
         return lower, upper
+
+    def own_diagonal(i, carry):
+        at = i + HALO_S
+        v = stiff[at]
+        zl, zu = z_sides(v)
+        rows = pl.ds(8, ny)
+        inner = v + up_y(v) + v + down_y(v)
+        inner = inner + v + jnp.where(cut_zl, v, zl) + v + jnp.where(cut_zu, v, zu)
+        inner = (inner + (2.0 + mass_share) * v)[8:8 + ny]
+        inner = inner + stiff[at - 1, rows, :] + stiff[at + 1, rows, :]
+        inv_d[i] = damping / inner
+        return carry
+
+    unrolled(0, nx, own_diagonal)
 
     def fine_weights(i, carry):
         at = i + HALO_S - 2
@@ -256,7 +278,6 @@
         d_ref[i] = diag
         return carry
 
-    lax.fori_loop(0, nx + 4, fine_weights, 0, unroll=2)
 
     cy = ey // 2
     ccut_row = lax.broadcasted_iota(jnp.int32, (cy, half), 0)
@@ -265,7 +286,6 @@
     ccut_yu = (ccut_row == 3 + ny // 2) & at_upper
     ccut_zl = ccut_lane == 0
     ccut_zu = ccut_lane == half - 1
-    ca_ref[...] = jnp.zeros_like(ca_ref)
 
     def coarse_weights(i, carry):
         def both(at):
@@ -305,7 +325,6 @@
         cd_ref[i, pl.ds(4, cy), :] = diag
         return carry
 
-    lax.fori_loop(0, nx // 2 + 6, coarse_weights, 0, unroll=2)
 
     for cond, lo_f, lo_c in ((at_lower, 0, 0), (at_upper, 8 + ny, 8 + ny // 2)):
         @pl.when(cond)
@@ -347,9 +366,13 @@
         even = jnp.where(low_lanes, first, pltpu.roll(second, half // 2, axis=1))
         odd = jnp.where(low_lanes, pltpu.roll(first, half // 2, axis=1), second)
         source = jnp.concatenate([even, odd], axis=1).reshape(nx, ny, nz)
-        diag = d_ref[pl.ds(2, nx), pl.ds(8, ny), :]
-        fine[c, pl.ds(HALO_F, nx), pl.ds(8, ny), :] = damping * source / diag
-        start(fine_copies[c])
+        fine[c, pl.ds(HALO_F, nx), pl.ds(8, ny), :] = source * inv_d[...]
+        start(fine_copies[c][0])
+
+    arrive(stiff_second)
+    ca_ref[...] = jnp.zeros_like(ca_ref)
+    lax.fori_loop(0, nx + 4, fine_weights, 0, unroll=2)
+    lax.fori_loop(0, nx // 2 + 6, coarse_weights, 0, unroll=2)
 
     def gathered(ref, at, weights, i):
         v = ref[at]
@@ -360,8 +383,8 @@
             + weights[4, i] * zl + weights[5, i] * zu
         )
 
-    for c in range(3):
-        finish(fine_copies[c])
+    def down(c):
+        arrive(fine_copies[c][1])
         f0, f1 = fine.at[c], fine1.at[c]
 
         def second_sweep(i, carry):
@@ -387,7 +410,7 @@
             return carry
 
         unrolled(0, nx // 2, restrict)
-        start(coarse_copies[c])
+        start(coarse_copies[c][0])
 
     def gathered_c(ref, at, i):
         v = ref[at]
@@ -400,8 +423,9 @@
 
     from_halves = as_bf16(wide_c == jnp.where(wide_r < half, 2 * wide_r, 2 * wide_r - (nz - 1)))
     cx = nx // 2
-    for c in range(3):
-        finish(coarse_copies[c])
+
+    def back_up(c):
+        arrive(coarse_copies[c][1])
         c1 = coarse.at[0, c]
         for sweep in range(3):
             old, new = coarse.at[sweep, c], coarse.at[sweep + 1, c]
@@ -443,6 +467,17 @@
 
         unrolled(0, nx, post2)
 
+    for copies, work in ((fine_copies, down), (coarse_copies, back_up)):
+        for c in range(4):
+            if c < 3:
+                arrive(copies[c][0])
+                start(copies[c][1])
+            if c > 0:
+                work(c - 1)
+
+    for first, second in [(stiff_first, stiff_second)] + fine_copies + coarse_copies:
+        sent(first)
+        sent(second)
     for c in range(3):
         for q in range(pairs):
             to_sib(q, c).wait_send()
@@ -484,6 +519,7 @@
             pltpu.VMEM((3, nx + 2 * HALO_F, ey, nz), f32),
             pltpu.VMEM((3, nx + 4, ey, nz), f32),
             pltpu.VMEM((4, 3, cx + 2 * HALO_C, ecy, half), f32),
+            pltpu.VMEM((nx, ny, nz), f32),
             pltpu.VMEM((6, nx + 4, ey, nz), f32),
             pltpu.VMEM((nx + 4, ey, nz), f32),
             pltpu.VMEM((6, cx + 6, ecy, half), f32),

time: 42.3 us -> 40.5 us (0.957)
  Pallas kernels: 37.9 us -> 36.5 us
    pallas_call x1, Pallas kernels: 37.9 us -> 36.5 us  [shards(): pl.pallas_call(functools.partial(kernel, passages, spans), out_shape=jax....]
where the time goes in v3:
time: 40.5 us; the launch traced here: 40.2 us
  Pallas kernels  36.5 us (90%)
  local copies, waits for them, and re-layouts  3.13 us (8%)
  other arithmetic  0.59 us (1%)
    pallas_call x1, Pallas kernels, shards(): pl.pallas_call(functools.partial(kernel, passages, spans), out_shape=jax....  36.5 us
    unnamed x5, local copies, waits for them, and re-layouts  3.13 us

profile of v3, /device:TPU:1, one launch (start us, length us, event | category | flops | bytes accessed | tf_op | source)
XLA Modules:
  0.0 40.2 jit_solution(9454643702838994268)
XLA Ops:
  0.0 0.0 copy-start.1
  0.0 0.7 %copy-done.1 = s32[512,1]{0,1:T(1,128)S(1)} copy-done((s32[512,1]{0,1:T(1,128)S(1)}, s32[512,1]{0,1:T(1,128)}, u32[]{:S(2)}) %copy-start.1) | copy-done | bytes 2072
  0.7 0.0 copy-start
  0.7 0.7 %copy-done = s32[512]{0:T(512)S(1)} copy-done((s32[512]{0:T(512)S(1)}, s32[512]{0:T(512)}, u32[]{:S(2)}) %copy-start) | copy-done | bytes 2072
  1.4 0.6 %fusion.2 = s32[512]{0:T(512)} fusion(s32[512]{0:T(512)S(1)} %bitcast.6, s32[512]{0:T(512)S(1)} %copy-done), kind=kLoop, calls=%fused_computation.7 | loop fusion | flops 11264 | bytes 6144 | tf_op jit(solution)/shard_map/add | solution.py:495
  2.0 36.5 %shard_map.55 = f32[3,8,16,256]{3,2,1,0:T(8,128)} custom-call(s32[1,512]{1,0:T(1,128)} %bitcast.5, f32[3,512,128]{2,1,0:T(8,128)} %bitcast.4, s32[8,16,256]{2,1,0:T(8,128)} %class_hbm.1, f32[1,16]{1,0:T(1,128)} %bitcast.7), custom_call_target="tpu_custom_call" | custom-call | tf_op jit(solution)/shard_map/pallas_call | solution.py:502
  38.5 1.8 %copy.7 = f32[3,8,16,256]{3,2,1,0:T(8,128)} copy(f32[3,8,16,256]{3,2,1,0:T(8,128)} %shard_map.55) | data formatting | bytes 786432
  (1 shorter events, 0.0 us)
Async XLA Ops:
  0.0 0.7 %copy-start.1 = (s32[512,1]{0,1:T(1,128)S(1)}, s32[512,1]{0,1:T(1,128)}, u32[]{:S(2)}) copy-start(s32[512,1]{0,1:T(1,128)} %param.6) | copy-start | bytes 6148
  0.7 0.7 %copy-start = (s32[512]{0:T(512)S(1)}, s32[512]{0:T(512)}, u32[]{:S(2)}) copy-start(s32[512]{0:T(512)} %param.7) | copy-start | bytes 6148
